TPU v7x, 32 devices: a whole 2x2x4 slice. The times are simulated.
32 devices in a mesh: groups: 2 (over y), loop: 16 (over z, x, core).
Axes of the slice: x: 2, y: 2, z: 4, core: 2. Of those that a mesh axis runs over, the one named last changes fastest.
Arguments:
- image_feats: bfloat16 [4096, 768], P(('groups', 'loop')), parts along dimension 0, may hold values from -4 to 4
- text_feats: bfloat16 [4096, 768], P(('groups', 'loop')), parts along dimension 0, may hold values from -4 to 4
- image_proj: bfloat16 [768, 256], replicated, may hold values from -0.12629537 to 0.12629537
- text_proj: bfloat16 [768, 256], replicated, may hold values from -0.12629537 to 0.12629537
- pair_ids: int32 [4096], P(('groups', 'loop')), parts along dimension 0, may hold values from 0 to 255
- log_temp: float32 [1], replicated, may hold values from 2.7 to 3
- bias: float32 [1], replicated, may hold values from -7 to -5.5
- loss_grad: float32 [1], replicated, may hold values from 8 to 24
Outputs:
- image_grad: bfloat16 [4096, 768], P(('groups', 'loop')), parts along dimension 0
- text_grad: bfloat16 [4096, 768], P(('groups', 'loop')), parts along dimension 0
- weight_grads: float32 [1536, 512], P(('groups', 'loop')), parts along dimension 0
There are 2 independent parts, one for each index of `groups`. A program takes and returns all parts, laid end to end along the dimension named above; an argument that names none is the same for every part. Nothing has to cross between parts.
All inputs are finite; a program needn't handle non-finite values.
Results may differ from a plain program's by a relative error of at most 0.0062.
Values may be sent and summed in bfloat16 or wider, within the bound.
A program may use at most 64 MiB of HBM per device.

v0:
```python
import jax
import jax.numpy as jnp
from jax import lax
from jax.sharding import PartitionSpec as P


def shifted(block, axis, distance):
    devices = range(lax.axis_size(axis))
    route = [((i - distance) % len(devices), i) for i in devices]
    return lax.ppermute(block, axis, route)


def unit_rows(raw):
    norm = jnp.sqrt(jnp.sum(raw * raw, axis=-1, keepdims=True) + 1e-06)
    return (raw / norm, norm)


def tile_term(own_half, own_ids, other_half, other_ids, temp, bias_v, scale):
    logits = temp * jnp.dot(own_half, other_half.T, preferred_element_type=jnp.float32) + bias_v
    equal = (own_ids[:, None] == other_ids[None, :]).astype(jnp.float32)
    coeff = (scale * (jax.nn.sigmoid(logits) - equal)).astype(jnp.bfloat16)
    return jnp.dot(coeff, other_half, preferred_element_type=jnp.float32)


def body(image_feats, text_feats, image_proj, text_proj, pair_ids, log_temp, bias, loss_grad):
    image_raw = jnp.dot(image_feats, image_proj, preferred_element_type=jnp.float32)
    text_raw = jnp.dot(text_feats, text_proj, preferred_element_type=jnp.float32)
    image_unit, image_norm = unit_rows(image_raw)
    text_unit, text_norm = unit_rows(text_raw)
    image_half = image_unit.astype(jnp.bfloat16)
    text_half = text_unit.astype(jnp.bfloat16)
    temp = jnp.exp(log_temp[0])
    bias_v = bias[0]
    scale = loss_grad[0]
    count = lax.axis_size("loop")

    def visit(accs, other_image, other_text, other_ids):
        image_acc = accs[0] + tile_term(
            image_half, pair_ids, other_text, other_ids, temp, bias_v, scale
        )
        text_acc = accs[1] + tile_term(
            text_half, pair_ids, other_image, other_ids, temp, bias_v, scale
        )
        return (image_acc, text_acc)

    zeros = jnp.zeros(image_raw.shape, jnp.float32)
    own = (image_half, text_half, pair_ids)
    first = visit((zeros, zeros), image_half, text_half, pair_ids)

    def cycle_step(step, state):
        moved = shifted((state[0][0], state[0][1], state[0][2]), "loop", 1)
        return (moved, visit(state[1], moved[0], moved[1], moved[2]))

    accs = lax.fori_loop(0, count - 1, cycle_step, (own, first))[1]
    image_unit_grad = temp * accs[0]
    text_unit_grad = temp * accs[1]
    image_raw_grad = (
        (
            image_unit_grad
            - image_unit * jnp.sum(image_unit * image_unit_grad, axis=-1, keepdims=True)
        )
        / image_norm
    ).astype(jnp.bfloat16)
    text_raw_grad = (
        (text_unit_grad - text_unit * jnp.sum(text_unit * text_unit_grad, axis=-1, keepdims=True))
        / text_norm
    ).astype(jnp.bfloat16)
    image_grad = jnp.dot(image_raw_grad, image_proj.T, preferred_element_type=jnp.float32).astype(
        jnp.bfloat16
    )
    text_grad = jnp.dot(text_raw_grad, text_proj.T, preferred_element_type=jnp.float32).astype(
        jnp.bfloat16
    )
    image_part = jnp.einsum(
        "re,rp->ep", image_feats, image_raw_grad, preferred_element_type=jnp.float32
    )
    text_part = jnp.einsum(
        "re,rp->ep", text_feats, text_raw_grad, preferred_element_type=jnp.float32
    )
    weight_grads = lax.psum_scatter(
        jnp.concatenate([image_part, text_part], axis=1), "loop", scatter_dimension=0, tiled=True
    )
    return (image_grad, text_grad, weight_grads)


def solution(mesh):
    placed = (
        P(("groups", "loop"), None),
        P(("groups", "loop"), None),
        P(),
        P(),
        P(("groups", "loop")),
        P(),
        P(),
        P(),
    )
    return jax.shard_map(
        body,
        mesh=mesh,
        in_specs=placed,
        out_specs=(
            P(("groups", "loop"), None),
            P(("groups", "loop"), None),
            P(("groups", "loop"), None),
        ),
        check_vma=False,
    )
```

profile of v0, /device:TPU:0, one launch (start us, length us, event | category | flops | bytes accessed | tf_op | source)
XLA Modules:
  0.0 239.4 jit_solution(7479447008258799312)
XLA Ops:
  13.5 158.9 %while.18 = (s32[]{:T(128)}, bf16[128,256]{1,0:T(8,128)(2,1)S(1)}, bf16[128,256]{1,0:T(8,128)(2,1)S(1)}, s32[128]{0:T(128)S(1)}, f32[128,256]{1,0:T(8,128)S(1)},...) while((s32[]{:T(128)}, bf16[128,256]{1,0:T(8,128)(2,1)S(1)}, ...), condition=%wide.region_3.0_spmd, body=%wide.region_2.0_spmd.sunk | while | flops 33947648 | bytes 1578253 | solution.py:54
  14.0 2.6 %collective-permute-start = (bf16[128,256]{1,0:T(8,128)(2,1)S(1)}, bf16[128,256]{1,0:T(8,128)(2,1)S(1)}, u32[]{:S(2)}, u32[]{:S(2)}) collective-permute-start(bf16[128,256]{1,0:T(8,128)(2,1)S(1)} %get-tuple-element.191), channel_id=1, source_target_pairs={{15,0},{0,1},{1,2},{2,3},{3,4},{4,5},{5,6},{6,7},{7,8},{8,9},{9,10... | collective-permute-start | bytes 196616 | tf_op jit(solution)/shard_map/while/body/eval_jaxpr/ppermute | solution.py:10
  16.7 5.6 %collective-permute-done.2 = s32[128]{0:T(128)S(1)} collective-permute-done((s32[128]{0:T(128)S(1)}, s32[128]{0:T(128)S(1)}, u32[]{:S(2)}, u32[]{:S(2)}) %collective-permute-start.2) | collective-permute-done | bytes 544 | tf_op jit(solution)/shard_map/while/body/eval_jaxpr/ppermute | solution.py:10
  22.3 1.6 convolution_add_fusion.4
  25.8 7.0 %collective-permute-done.2 = s32[128]{0:T(128)S(1)} collective-permute-done((s32[128]{0:T(128)S(1)}, s32[128]{0:T(128)S(1)}, u32[]{:S(2)}, u32[]{:S(2)}) %collective-permute-start.2) | collective-permute-done | bytes 544 | tf_op jit(solution)/shard_map/while/body/eval_jaxpr/ppermute | solution.py:10
  32.8 1.6 convolution_add_fusion.4
  34.4 1.6 convolution_add_fusion.5
  36.3 7.0 %collective-permute-done.2 = s32[128]{0:T(128)S(1)} collective-permute-done((s32[128]{0:T(128)S(1)}, s32[128]{0:T(128)S(1)}, u32[]{:S(2)}, u32[]{:S(2)}) %collective-permute-start.2) | collective-permute-done | bytes 544 | tf_op jit(solution)/shard_map/while/body/eval_jaxpr/ppermute | solution.py:10
  43.3 1.6 convolution_add_fusion.4
  46.8 7.0 %collective-permute-done.2 = s32[128]{0:T(128)S(1)} collective-permute-done((s32[128]{0:T(128)S(1)}, s32[128]{0:T(128)S(1)}, u32[]{:S(2)}, u32[]{:S(2)}) %collective-permute-start.2) | collective-permute-done | bytes 544 | tf_op jit(solution)/shard_map/while/body/eval_jaxpr/ppermute | solution.py:10
  55.4 1.6 convolution_add_fusion.5
  57.2 7.0 %collective-permute-done.2 = s32[128]{0:T(128)S(1)} collective-permute-done((s32[128]{0:T(128)S(1)}, s32[128]{0:T(128)S(1)}, u32[]{:S(2)}, u32[]{:S(2)}) %collective-permute-start.2) | collective-permute-done | bytes 544 | tf_op jit(solution)/shard_map/while/body/eval_jaxpr/ppermute | solution.py:10
  64.3 1.6 convolution_add_fusion.4
  65.9 1.6 convolution_add_fusion.5
  67.7 7.0 %collective-permute-done.2 = s32[128]{0:T(128)S(1)} collective-permute-done((s32[128]{0:T(128)S(1)}, s32[128]{0:T(128)S(1)}, u32[]{:S(2)}, u32[]{:S(2)}) %collective-permute-start.2) | collective-permute-done | bytes 544 | tf_op jit(solution)/shard_map/while/body/eval_jaxpr/ppermute | solution.py:10
  74.8 1.6 convolution_add_fusion.4
  78.2 7.0 %collective-permute-done.2 = s32[128]{0:T(128)S(1)} collective-permute-done((s32[128]{0:T(128)S(1)}, s32[128]{0:T(128)S(1)}, u32[]{:S(2)}, u32[]{:S(2)}) %collective-permute-start.2) | collective-permute-done | bytes 544 | tf_op jit(solution)/shard_map/while/body/eval_jaxpr/ppermute | solution.py:10
  85.3 1.6 convolution_add_fusion.4
  88.7 7.0 %collective-permute-done.2 = s32[128]{0:T(128)S(1)} collective-permute-done((s32[128]{0:T(128)S(1)}, s32[128]{0:T(128)S(1)}, u32[]{:S(2)}, u32[]{:S(2)}) %collective-permute-start.2) | collective-permute-done | bytes 544 | tf_op jit(solution)/shard_map/while/body/eval_jaxpr/ppermute | solution.py:10
  97.4 1.6 convolution_add_fusion.5
  99.2 7.0 %collective-permute-done.2 = s32[128]{0:T(128)S(1)} collective-permute-done((s32[128]{0:T(128)S(1)}, s32[128]{0:T(128)S(1)}, u32[]{:S(2)}, u32[]{:S(2)}) %collective-permute-start.2) | collective-permute-done | bytes 544 | tf_op jit(solution)/shard_map/while/body/eval_jaxpr/ppermute | solution.py:10
  106.3 1.6 convolution_add_fusion.4
  107.9 1.6 convolution_add_fusion.5
  109.7 7.0 %collective-permute-done.2 = s32[128]{0:T(128)S(1)} collective-permute-done((s32[128]{0:T(128)S(1)}, s32[128]{0:T(128)S(1)}, u32[]{:S(2)}, u32[]{:S(2)}) %collective-permute-start.2) | collective-permute-done | bytes 544 | tf_op jit(solution)/shard_map/while/body/eval_jaxpr/ppermute | solution.py:10
  116.8 1.6 convolution_add_fusion.4
  120.2 7.0 %collective-permute-done.2 = s32[128]{0:T(128)S(1)} collective-permute-done((s32[128]{0:T(128)S(1)}, s32[128]{0:T(128)S(1)}, u32[]{:S(2)}, u32[]{:S(2)}) %collective-permute-start.2) | collective-permute-done | bytes 544 | tf_op jit(solution)/shard_map/while/body/eval_jaxpr/ppermute | solution.py:10
  130.7 7.0 %collective-permute-done.2 = s32[128]{0:T(128)S(1)} collective-permute-done((s32[128]{0:T(128)S(1)}, s32[128]{0:T(128)S(1)}, u32[]{:S(2)}, u32[]{:S(2)}) %collective-permute-start.2) | collective-permute-done | bytes 544 | tf_op jit(solution)/shard_map/while/body/eval_jaxpr/ppermute | solution.py:10
  141.2 7.0 %collective-permute-done.2 = s32[128]{0:T(128)S(1)} collective-permute-done((s32[128]{0:T(128)S(1)}, s32[128]{0:T(128)S(1)}, u32[]{:S(2)}, u32[]{:S(2)}) %collective-permute-start.2) | collective-permute-done | bytes 544 | tf_op jit(solution)/shard_map/while/body/eval_jaxpr/ppermute | solution.py:10
  151.7 7.0 %collective-permute-done.2 = s32[128]{0:T(128)S(1)} collective-permute-done((s32[128]{0:T(128)S(1)}, s32[128]{0:T(128)S(1)}, u32[]{:S(2)}, u32[]{:S(2)}) %collective-permute-start.2) | collective-permute-done | bytes 544 | tf_op jit(solution)/shard_map/while/body/eval_jaxpr/ppermute | solution.py:10
  162.2 7.0 %collective-permute-done.2 = s32[128]{0:T(128)S(1)} collective-permute-done((s32[128]{0:T(128)S(1)}, s32[128]{0:T(128)S(1)}, u32[]{:S(2)}, u32[]{:S(2)}) %collective-permute-start.2) | collective-permute-done | bytes 544 | tf_op jit(solution)/shard_map/while/body/eval_jaxpr/ppermute | solution.py:10
  173.9 1.6 copy.13
  177.5 55.0 %reduce-scatter.4.cloned.1.call-done = f32[48,512]{1,0:T(8,128)} async-done(((f32[768,512]{1,0:T(8,128)}), f32[48,512]{1,0:T(8,128)}) %reduce-scatter.4.cloned.1.call-update) | async-done | bytes 98320
  (165 shorter events, 38.2 us)
Async XLA Ops:
  7.2 225.3 %reduce-scatter.4.cloned.1.call-start = ((), (), s32[]{:S(2)}) async-start(), calls=%async_computation.1 | async-start | bytes 1671168
  13.5 8.8 %collective-permute-start.1 = (bf16[128,256]{1,0:T(8,128)(2,1)S(1)}, bf16[128,256]{1,0:T(8,128)(2,1)S(1)}, u32[]{:S(2)}, u32[]{:S(2)}) collective-permute-start(bf16[128,256]{1,0:T(8,128)(2,1)S(1)} %get-tuple-element.192), channel_id=1, source_target_pairs={{15,0},{0,1},{1,2},{2,3},{3,4},{4,5},{5,6},{6,7},{7,8},{8,9},{9,10... | collective-permute-start | bytes 196616 | tf_op jit(solution)/shard_map/while/body/eval_jaxpr/ppermute | solution.py:10
  14.0 8.3 %collective-permute-start = (bf16[128,256]{1,0:T(8,128)(2,1)S(1)}, bf16[128,256]{1,0:T(8,128)(2,1)S(1)}, u32[]{:S(2)}, u32[]{:S(2)}) collective-permute-start(bf16[128,256]{1,0:T(8,128)(2,1)S(1)} %get-tuple-element.191), channel_id=1, source_target_pairs={{15,0},{0,1},{1,2},{2,3},{3,4},{4,5},{5,6},{6,7},{7,8},{8,9},{9,10... | collective-permute-start | bytes 196616 | tf_op jit(solution)/shard_map/while/body/eval_jaxpr/ppermute | solution.py:10
  25.6 7.2 %collective-permute-start.1 = (bf16[128,256]{1,0:T(8,128)(2,1)S(1)}, bf16[128,256]{1,0:T(8,128)(2,1)S(1)}, u32[]{:S(2)}, u32[]{:S(2)}) collective-permute-start(bf16[128,256]{1,0:T(8,128)(2,1)S(1)} %get-tuple-element.192), channel_id=1, source_target_pairs={{15,0},{0,1},{1,2},{2,3},{3,4},{4,5},{5,6},{6,7},{7,8},{8,9},{9,10... | collective-permute-start | bytes 196616 | tf_op jit(solution)/shard_map/while/body/eval_jaxpr/ppermute | solution.py:10
  25.6 7.2 %collective-permute-start = (bf16[128,256]{1,0:T(8,128)(2,1)S(1)}, bf16[128,256]{1,0:T(8,128)(2,1)S(1)}, u32[]{:S(2)}, u32[]{:S(2)}) collective-permute-start(bf16[128,256]{1,0:T(8,128)(2,1)S(1)} %get-tuple-element.191), channel_id=1, source_target_pairs={{15,0},{0,1},{1,2},{2,3},{3,4},{4,5},{5,6},{6,7},{7,8},{8,9},{9,10... | collective-permute-start | bytes 196616 | tf_op jit(solution)/shard_map/while/body/eval_jaxpr/ppermute | solution.py:10
  25.7 7.1 %collective-permute-start.2 = (s32[128]{0:T(128)S(1)}, s32[128]{0:T(128)S(1)}, u32[]{:S(2)}, u32[]{:S(2)}) collective-permute-start(s32[128]{0:T(128)S(1)} %get-tuple-element.193), channel_id=1, source_target_pairs={{15,0},{0,1},{1,2},{2,3},{3,4},{4,5},{5,6},{6,7},{7,8},{8,9},{9,10... | collective-permute-start | bytes 1544 | tf_op jit(solution)/shard_map/while/body/eval_jaxpr/ppermute | solution.py:10
  36.1 7.2 %collective-permute-start.1 = (bf16[128,256]{1,0:T(8,128)(2,1)S(1)}, bf16[128,256]{1,0:T(8,128)(2,1)S(1)}, u32[]{:S(2)}, u32[]{:S(2)}) collective-permute-start(bf16[128,256]{1,0:T(8,128)(2,1)S(1)} %get-tuple-element.192), channel_id=1, source_target_pairs={{15,0},{0,1},{1,2},{2,3},{3,4},{4,5},{5,6},{6,7},{7,8},{8,9},{9,10... | collective-permute-start | bytes 196616 | tf_op jit(solution)/shard_map/while/body/eval_jaxpr/ppermute | solution.py:10
  36.1 7.2 %collective-permute-start = (bf16[128,256]{1,0:T(8,128)(2,1)S(1)}, bf16[128,256]{1,0:T(8,128)(2,1)S(1)}, u32[]{:S(2)}, u32[]{:S(2)}) collective-permute-start(bf16[128,256]{1,0:T(8,128)(2,1)S(1)} %get-tuple-element.191), channel_id=1, source_target_pairs={{15,0},{0,1},{1,2},{2,3},{3,4},{4,5},{5,6},{6,7},{7,8},{8,9},{9,10... | collective-permute-start | bytes 196616 | tf_op jit(solution)/shard_map/while/body/eval_jaxpr/ppermute | solution.py:10
  46.6 7.2 %collective-permute-start.1 = (bf16[128,256]{1,0:T(8,128)(2,1)S(1)}, bf16[128,256]{1,0:T(8,128)(2,1)S(1)}, u32[]{:S(2)}, u32[]{:S(2)}) collective-permute-start(bf16[128,256]{1,0:T(8,128)(2,1)S(1)} %get-tuple-element.192), channel_id=1, source_target_pairs={{15,0},{0,1},{1,2},{2,3},{3,4},{4,5},{5,6},{6,7},{7,8},{8,9},{9,10... | collective-permute-start | bytes 196616 | tf_op jit(solution)/shard_map/while/body/eval_jaxpr/ppermute | solution.py:10
  46.6 7.2 %collective-permute-start = (bf16[128,256]{1,0:T(8,128)(2,1)S(1)}, bf16[128,256]{1,0:T(8,128)(2,1)S(1)}, u32[]{:S(2)}, u32[]{:S(2)}) collective-permute-start(bf16[128,256]{1,0:T(8,128)(2,1)S(1)} %get-tuple-element.191), channel_id=1, source_target_pairs={{15,0},{0,1},{1,2},{2,3},{3,4},{4,5},{5,6},{6,7},{7,8},{8,9},{9,10... | collective-permute-start | bytes 196616 | tf_op jit(solution)/shard_map/while/body/eval_jaxpr/ppermute | solution.py:10
  57.0 7.2 %collective-permute-start.1 = (bf16[128,256]{1,0:T(8,128)(2,1)S(1)}, bf16[128,256]{1,0:T(8,128)(2,1)S(1)}, u32[]{:S(2)}, u32[]{:S(2)}) collective-permute-start(bf16[128,256]{1,0:T(8,128)(2,1)S(1)} %get-tuple-element.192), channel_id=1, source_target_pairs={{15,0},{0,1},{1,2},{2,3},{3,4},{4,5},{5,6},{6,7},{7,8},{8,9},{9,10... | collective-permute-start | bytes 196616 | tf_op jit(solution)/shard_map/while/body/eval_jaxpr/ppermute | solution.py:10
  57.1 7.2 %collective-permute-start = (bf16[128,256]{1,0:T(8,128)(2,1)S(1)}, bf16[128,256]{1,0:T(8,128)(2,1)S(1)}, u32[]{:S(2)}, u32[]{:S(2)}) collective-permute-start(bf16[128,256]{1,0:T(8,128)(2,1)S(1)} %get-tuple-element.191), channel_id=1, source_target_pairs={{15,0},{0,1},{1,2},{2,3},{3,4},{4,5},{5,6},{6,7},{7,8},{8,9},{9,10... | collective-permute-start | bytes 196616 | tf_op jit(solution)/shard_map/while/body/eval_jaxpr/ppermute | solution.py:10
  67.5 7.2 %collective-permute-start.1 = (bf16[128,256]{1,0:T(8,128)(2,1)S(1)}, bf16[128,256]{1,0:T(8,128)(2,1)S(1)}, u32[]{:S(2)}, u32[]{:S(2)}) collective-permute-start(bf16[128,256]{1,0:T(8,128)(2,1)S(1)} %get-tuple-element.192), channel_id=1, source_target_pairs={{15,0},{0,1},{1,2},{2,3},{3,4},{4,5},{5,6},{6,7},{7,8},{8,9},{9,10... | collective-permute-start | bytes 196616 | tf_op jit(solution)/shard_map/while/body/eval_jaxpr/ppermute | solution.py:10
  67.6 7.2 %collective-permute-start = (bf16[128,256]{1,0:T(8,128)(2,1)S(1)}, bf16[128,256]{1,0:T(8,128)(2,1)S(1)}, u32[]{:S(2)}, u32[]{:S(2)}) collective-permute-start(bf16[128,256]{1,0:T(8,128)(2,1)S(1)} %get-tuple-element.191), channel_id=1, source_target_pairs={{15,0},{0,1},{1,2},{2,3},{3,4},{4,5},{5,6},{6,7},{7,8},{8,9},{9,10... | collective-permute-start | bytes 196616 | tf_op jit(solution)/shard_map/while/body/eval_jaxpr/ppermute | solution.py:10
  78.0 7.2 %collective-permute-start.1 = (bf16[128,256]{1,0:T(8,128)(2,1)S(1)}, bf16[128,256]{1,0:T(8,128)(2,1)S(1)}, u32[]{:S(2)}, u32[]{:S(2)}) collective-permute-start(bf16[128,256]{1,0:T(8,128)(2,1)S(1)} %get-tuple-element.192), channel_id=1, source_target_pairs={{15,0},{0,1},{1,2},{2,3},{3,4},{4,5},{5,6},{6,7},{7,8},{8,9},{9,10... | collective-permute-start | bytes 196616 | tf_op jit(solution)/shard_map/while/body/eval_jaxpr/ppermute | solution.py:10
  78.1 7.2 %collective-permute-start = (bf16[128,256]{1,0:T(8,128)(2,1)S(1)}, bf16[128,256]{1,0:T(8,128)(2,1)S(1)}, u32[]{:S(2)}, u32[]{:S(2)}) collective-permute-start(bf16[128,256]{1,0:T(8,128)(2,1)S(1)} %get-tuple-element.191), channel_id=1, source_target_pairs={{15,0},{0,1},{1,2},{2,3},{3,4},{4,5},{5,6},{6,7},{7,8},{8,9},{9,10... | collective-permute-start | bytes 196616 | tf_op jit(solution)/shard_map/while/body/eval_jaxpr/ppermute | solution.py:10
  88.5 7.2 %collective-permute-start.1 = (bf16[128,256]{1,0:T(8,128)(2,1)S(1)}, bf16[128,256]{1,0:T(8,128)(2,1)S(1)}, u32[]{:S(2)}, u32[]{:S(2)}) collective-permute-start(bf16[128,256]{1,0:T(8,128)(2,1)S(1)} %get-tuple-element.192), channel_id=1, source_target_pairs={{15,0},{0,1},{1,2},{2,3},{3,4},{4,5},{5,6},{6,7},{7,8},{8,9},{9,10... | collective-permute-start | bytes 196616 | tf_op jit(solution)/shard_map/while/body/eval_jaxpr/ppermute | solution.py:10
  88.6 7.2 %collective-permute-start = (bf16[128,256]{1,0:T(8,128)(2,1)S(1)}, bf16[128,256]{1,0:T(8,128)(2,1)S(1)}, u32[]{:S(2)}, u32[]{:S(2)}) collective-permute-start(bf16[128,256]{1,0:T(8,128)(2,1)S(1)} %get-tuple-element.191), channel_id=1, source_target_pairs={{15,0},{0,1},{1,2},{2,3},{3,4},{4,5},{5,6},{6,7},{7,8},{8,9},{9,10... | collective-permute-start | bytes 196616 | tf_op jit(solution)/shard_map/while/body/eval_jaxpr/ppermute | solution.py:10
  99.0 7.2 %collective-permute-start.1 = (bf16[128,256]{1,0:T(8,128)(2,1)S(1)}, bf16[128,256]{1,0:T(8,128)(2,1)S(1)}, u32[]{:S(2)}, u32[]{:S(2)}) collective-permute-start(bf16[128,256]{1,0:T(8,128)(2,1)S(1)} %get-tuple-element.192), channel_id=1, source_target_pairs={{15,0},{0,1},{1,2},{2,3},{3,4},{4,5},{5,6},{6,7},{7,8},{8,9},{9,10... | collective-permute-start | bytes 196616 | tf_op jit(solution)/shard_map/while/body/eval_jaxpr/ppermute | solution.py:10
  99.1 7.2 %collective-permute-start = (bf16[128,256]{1,0:T(8,128)(2,1)S(1)}, bf16[128,256]{1,0:T(8,128)(2,1)S(1)}, u32[]{:S(2)}, u32[]{:S(2)}) collective-permute-start(bf16[128,256]{1,0:T(8,128)(2,1)S(1)} %get-tuple-element.191), channel_id=1, source_target_pairs={{15,0},{0,1},{1,2},{2,3},{3,4},{4,5},{5,6},{6,7},{7,8},{8,9},{9,10... | collective-permute-start | bytes 196616 | tf_op jit(solution)/shard_map/while/body/eval_jaxpr/ppermute | solution.py:10
  109.5 7.2 %collective-permute-start.1 = (bf16[128,256]{1,0:T(8,128)(2,1)S(1)}, bf16[128,256]{1,0:T(8,128)(2,1)S(1)}, u32[]{:S(2)}, u32[]{:S(2)}) collective-permute-start(bf16[128,256]{1,0:T(8,128)(2,1)S(1)} %get-tuple-element.192), channel_id=1, source_target_pairs={{15,0},{0,1},{1,2},{2,3},{3,4},{4,5},{5,6},{6,7},{7,8},{8,9},{9,10... | collective-permute-start | bytes 196616 | tf_op jit(solution)/shard_map/while/body/eval_jaxpr/ppermute | solution.py:10
  109.6 7.2 %collective-permute-start = (bf16[128,256]{1,0:T(8,128)(2,1)S(1)}, bf16[128,256]{1,0:T(8,128)(2,1)S(1)}, u32[]{:S(2)}, u32[]{:S(2)}) collective-permute-start(bf16[128,256]{1,0:T(8,128)(2,1)S(1)} %get-tuple-element.191), channel_id=1, source_target_pairs={{15,0},{0,1},{1,2},{2,3},{3,4},{4,5},{5,6},{6,7},{7,8},{8,9},{9,10... | collective-permute-start | bytes 196616 | tf_op jit(solution)/shard_map/while/body/eval_jaxpr/ppermute | solution.py:10
  120.0 7.2 %collective-permute-start.1 = (bf16[128,256]{1,0:T(8,128)(2,1)S(1)}, bf16[128,256]{1,0:T(8,128)(2,1)S(1)}, u32[]{:S(2)}, u32[]{:S(2)}) collective-permute-start(bf16[128,256]{1,0:T(8,128)(2,1)S(1)} %get-tuple-element.192), channel_id=1, source_target_pairs={{15,0},{0,1},{1,2},{2,3},{3,4},{4,5},{5,6},{6,7},{7,8},{8,9},{9,10... | collective-permute-start | bytes 196616 | tf_op jit(solution)/shard_map/while/body/eval_jaxpr/ppermute | solution.py:10
  120.1 7.2 %collective-permute-start = (bf16[128,256]{1,0:T(8,128)(2,1)S(1)}, bf16[128,256]{1,0:T(8,128)(2,1)S(1)}, u32[]{:S(2)}, u32[]{:S(2)}) collective-permute-start(bf16[128,256]{1,0:T(8,128)(2,1)S(1)} %get-tuple-element.191), channel_id=1, source_target_pairs={{15,0},{0,1},{1,2},{2,3},{3,4},{4,5},{5,6},{6,7},{7,8},{8,9},{9,10... | collective-permute-start | bytes 196616 | tf_op jit(solution)/shard_map/while/body/eval_jaxpr/ppermute | solution.py:10
  130.5 7.2 %collective-permute-start.1 = (bf16[128,256]{1,0:T(8,128)(2,1)S(1)}, bf16[128,256]{1,0:T(8,128)(2,1)S(1)}, u32[]{:S(2)}, u32[]{:S(2)}) collective-permute-start(bf16[128,256]{1,0:T(8,128)(2,1)S(1)} %get-tuple-element.192), channel_id=1, source_target_pairs={{15,0},{0,1},{1,2},{2,3},{3,4},{4,5},{5,6},{6,7},{7,8},{8,9},{9,10... | collective-permute-start | bytes 196616 | tf_op jit(solution)/shard_map/while/body/eval_jaxpr/ppermute | solution.py:10
  130.6 7.2 %collective-permute-start = (bf16[128,256]{1,0:T(8,128)(2,1)S(1)}, bf16[128,256]{1,0:T(8,128)(2,1)S(1)}, u32[]{:S(2)}, u32[]{:S(2)}) collective-permute-start(bf16[128,256]{1,0:T(8,128)(2,1)S(1)} %get-tuple-element.191), channel_id=1, source_target_pairs={{15,0},{0,1},{1,2},{2,3},{3,4},{4,5},{5,6},{6,7},{7,8},{8,9},{9,10... | collective-permute-start | bytes 196616 | tf_op jit(solution)/shard_map/while/body/eval_jaxpr/ppermute | solution.py:10
  141.0 7.2 %collective-permute-start.1 = (bf16[128,256]{1,0:T(8,128)(2,1)S(1)}, bf16[128,256]{1,0:T(8,128)(2,1)S(1)}, u32[]{:S(2)}, u32[]{:S(2)}) collective-permute-start(bf16[128,256]{1,0:T(8,128)(2,1)S(1)} %get-tuple-element.192), channel_id=1, source_target_pairs={{15,0},{0,1},{1,2},{2,3},{3,4},{4,5},{5,6},{6,7},{7,8},{8,9},{9,10... | collective-permute-start | bytes 196616 | tf_op jit(solution)/shard_map/while/body/eval_jaxpr/ppermute | solution.py:10
  141.1 7.2 %collective-permute-start = (bf16[128,256]{1,0:T(8,128)(2,1)S(1)}, bf16[128,256]{1,0:T(8,128)(2,1)S(1)}, u32[]{:S(2)}, u32[]{:S(2)}) collective-permute-start(bf16[128,256]{1,0:T(8,128)(2,1)S(1)} %get-tuple-element.191), channel_id=1, source_target_pairs={{15,0},{0,1},{1,2},{2,3},{3,4},{4,5},{5,6},{6,7},{7,8},{8,9},{9,10... | collective-permute-start | bytes 196616 | tf_op jit(solution)/shard_map/while/body/eval_jaxpr/ppermute | solution.py:10
  151.5 7.2 %collective-permute-start.1 = (bf16[128,256]{1,0:T(8,128)(2,1)S(1)}, bf16[128,256]{1,0:T(8,128)(2,1)S(1)}, u32[]{:S(2)}, u32[]{:S(2)}) collective-permute-start(bf16[128,256]{1,0:T(8,128)(2,1)S(1)} %get-tuple-element.192), channel_id=1, source_target_pairs={{15,0},{0,1},{1,2},{2,3},{3,4},{4,5},{5,6},{6,7},{7,8},{8,9},{9,10... | collective-permute-start | bytes 196616 | tf_op jit(solution)/shard_map/while/body/eval_jaxpr/ppermute | solution.py:10
  151.5 7.2 %collective-permute-start = (bf16[128,256]{1,0:T(8,128)(2,1)S(1)}, bf16[128,256]{1,0:T(8,128)(2,1)S(1)}, u32[]{:S(2)}, u32[]{:S(2)}) collective-permute-start(bf16[128,256]{1,0:T(8,128)(2,1)S(1)} %get-tuple-element.191), channel_id=1, source_target_pairs={{15,0},{0,1},{1,2},{2,3},{3,4},{4,5},{5,6},{6,7},{7,8},{8,9},{9,10... | collective-permute-start | bytes 196616 | tf_op jit(solution)/shard_map/while/body/eval_jaxpr/ppermute | solution.py:10
  162.0 7.2 %collective-permute-start.1 = (bf16[128,256]{1,0:T(8,128)(2,1)S(1)}, bf16[128,256]{1,0:T(8,128)(2,1)S(1)}, u32[]{:S(2)}, u32[]{:S(2)}) collective-permute-start(bf16[128,256]{1,0:T(8,128)(2,1)S(1)} %get-tuple-element.192), channel_id=1, source_target_pairs={{15,0},{0,1},{1,2},{2,3},{3,4},{4,5},{5,6},{6,7},{7,8},{8,9},{9,10... | collective-permute-start | bytes 196616 | tf_op jit(solution)/shard_map/while/body/eval_jaxpr/ppermute | solution.py:10
  162.0 7.2 %collective-permute-start = (bf16[128,256]{1,0:T(8,128)(2,1)S(1)}, bf16[128,256]{1,0:T(8,128)(2,1)S(1)}, u32[]{:S(2)}, u32[]{:S(2)}) collective-permute-start(bf16[128,256]{1,0:T(8,128)(2,1)S(1)} %get-tuple-element.191), channel_id=1, source_target_pairs={{15,0},{0,1},{1,2},{2,3},{3,4},{4,5},{5,6},{6,7},{7,8},{8,9},{9,10... | collective-permute-start | bytes 196616 | tf_op jit(solution)/shard_map/while/body/eval_jaxpr/ppermute | solution.py:10
  (19 other events, 268.7 us)
Sparse Core Ops, SparseCore 0:
  175.6 56.8 reduce-scatter.3
where the time goes:
time: 240 us; the launch traced here: 239 us
  waiting for transfers between devices  159 us (66%)
  matrix products  54.2 us (23%)
  between operations  16.2 us (7%)
  starting transfers between devices  5.64 us (2%)
  local copies, waits for them, and re-layouts  2.86 us (1%)
    ppermute x45, waiting for transfers between devices, shifted(): return lax.ppermute(block, axis, route)  104 us
    unnamed x2, waiting for transfers between devices  55.1 us
    dot_general x32, matrix products, tile_term(): return jnp.dot(coeff, other_half, preferred_element_type=jnp.float32)  48.9 us
    ppermute x45, starting transfers between devices, shifted(): return lax.ppermute(block, axis, route)  5.61 us
  transfers between devices with their start and end apart: 46, of which 16 were waited for; matrix products, arithmetic and copies ran while one was open for 1% of the time, Pallas kernels for 0%

commit v1 on v0

v1 whole, which is shorter than its diff:
```python
import functools

import jax
import jax.numpy as jnp
from jax import lax
from jax.experimental import pallas as pl
from jax.experimental.pallas import tpu as pltpu
from jax.sharding import PartitionSpec as P

B = 4
F32 = jnp.float32
BF16 = jnp.bfloat16


def dot(x, y, dims):
    return lax.dot_general(x, y, (dims, ((), ())), preferred_element_type=F32)


def unit_rows(raw):
    norm = jnp.sqrt(jnp.sum(raw * raw, axis=-1, keepdims=True) + 1e-06)
    return raw / norm, norm


def raw_grad_of(unit, norm, unit_grad):
    along = jnp.sum(unit * unit_grad, axis=-1, keepdims=True)
    return ((unit_grad - unit * along) / norm).astype(BF16)


def kernel(
    n, scatter,
    log_temp, bias, loss_grad, image_feats, text_feats, image_proj, text_proj, ids,
    image_grad, text_grad, weight_out,
    image_all, text_all, image_ids, text_ids, image_out, image_back, text_out, text_back,
    parts, core_in, core_sum, x_in, x_sum, z_in,
    image_sems, text_sems, image_id_sems, text_id_sems, image_back_sems, text_back_sems,
    core_sems, x_sems, z_sems,
):
    A = n // B
    rows = image_feats.shape[0]
    me = lax.axis_index("loop")
    a, b = me // B, me % B
    x, c = b // 2, b % 2
    near = [a * B + (b + k) % B for k in range(B)]
    near_back = [a * B + (b + B - k) % B for k in range(B)]
    far = [(a + k) % A * B + b for k in range(A)]
    far_back = [(a + A - k) % A * B + b for k in range(A)]
    core_peer = a * B + x * 2 + (1 - c)
    x_peer = a * B + (1 - x) * 2 + c

    def copy(src, dst, sems, where, to):
        return pltpu.make_async_remote_copy(
            src_ref=src, dst_ref=dst, send_sem=sems.at[(0,) + where], recv_sem=sems.at[(1,) + where],
            device_id={"loop": to}, device_id_type=pl.DeviceIdType.MESH,
        )

    barrier = pltpu.get_barrier_semaphore()
    for to in near[1:] + far[1:]:
        pl.semaphore_signal(
            barrier, inc=1, device_id={"loop": to}, device_id_type=pl.DeviceIdType.MESH
        )

    temp = jnp.exp(jnp.full((1, 1), log_temp[0], F32))
    bias_v = bias[0]
    scale = loss_grad[0]

    image_unit, image_norm = unit_rows(dot(image_feats[...], image_proj[...], ((1,), (0,))))
    image_all[0] = image_unit.astype(BF16)
    text_unit, text_norm = unit_rows(dot(text_feats[...], text_proj[...], ((1,), (0,))))
    text_all[0] = text_unit.astype(BF16)
    image_ids[0] = ids[...]
    text_ids[0] = ids[...]
    pl.semaphore_wait(barrier, A + B - 2)

    sent = []
    image_copies, text_copies, image_id_copies, text_id_copies = {}, {}, {}, {}
    for k in range(1, A):
        text_copies[k] = copy(text_all.at[0], text_all.at[k], text_sems, (k,), far[k])
        text_copies[k].start()
    for k in range(1, B):
        image_copies[k] = copy(image_all.at[0], image_all.at[k], image_sems, (k,), near[k])
        image_copies[k].start()
    for k in range(1, B):
        image_id_copies[k] = copy(image_ids.at[0], image_ids.at[k], image_id_sems, (k,), near[k])
        image_id_copies[k].start()
    for k in range(1, A):
        text_id_copies[k] = copy(text_ids.at[0], text_ids.at[k], text_id_sems, (k,), far[k])
        text_id_copies[k].start()
    sent += [*text_copies.values(), *image_copies.values()]
    sent += [*image_id_copies.values(), *text_id_copies.values()]

    for k in range(1, B):
        image_copies[k].wait_recv()
        image_id_copies[k].wait_recv()
    images = image_all[...].reshape(B * rows, image_all.shape[2])
    image_keys = jnp.concatenate(
        [jnp.broadcast_to(image_ids[k].astype(F32), (rows, rows)).T for k in range(B)], axis=0
    )

    image_acc = None
    text_own = None
    back = {}
    for k in [0, *range(1, A)]:
        if k:
            text_copies[k].wait_recv()
            text_id_copies[k].wait_recv()
        texts = text_all[k]
        logits = temp * dot(images, texts, ((1,), (1,))) + bias_v
        equal = (image_keys == text_ids[k].astype(F32)).astype(F32)
        coeff = (scale * (jax.nn.sigmoid(logits) - equal)).astype(BF16)
        term = dot(coeff, images, ((0,), (0,)))
        if k:
            text_out[k] = term.astype(BF16)
            back[k] = copy(text_out.at[k], text_back.at[k], text_back_sems, (k,), far_back[k])
            back[k].start()
        else:
            text_own = term
        term = dot(coeff, texts, ((1,), (0,)))
        image_acc = term if image_acc is None else image_acc + term
    sent += back.values()

    image_back_copies = {}
    for k in range(1, B):
        image_out[k] = image_acc[k * rows:(k + 1) * rows].astype(BF16)
        image_back_copies[k] = copy(
            image_out.at[k], image_back.at[k], image_back_sems, (k,), near_back[k]
        )
        image_back_copies[k].start()
    sent += image_back_copies.values()

    def reduced(own, copies, ref):
        total = own
        for k in copies:
            copies[k].wait_recv()
            total = total + ref[k].astype(F32)
        return temp * total

    sides = (
        (text_feats, text_unit, text_norm, text_own, back, text_back, text_proj, text_grad, 1),
        (image_feats, image_unit, image_norm, image_acc[:rows], image_back_copies, image_back,
         image_proj, image_grad, 0),
    )
    width = image_all.shape[2]
    raws = []
    core_copies = []
    for s, (feats, unit, norm, own, copies, ref, _, _, column) in enumerate(sides):
        raw = raw_grad_of(unit, norm, reduced(own, copies, ref))
        raws.append(raw)
        part = dot(feats[...], raw, ((0,), (0,)))
        if scatter:
            parts[s] = part.astype(BF16).reshape(parts.shape[1:])
            core_copies.append(
                copy(parts.at[s, :, :, 1 - c], core_in.at[s], core_sems, (s,), core_peer)
            )
            core_copies[s].start()
        else:
            weight_out[:, column * width:(column + 1) * width] = part

    def grad(s):
        proj, out = sides[s][6:8]
        out[...] = dot(raws[s], proj[...], ((1,), (1,))).astype(BF16)

    if not scatter:
        grad(0)
        grad(1)
    else:
        x_copies, z_copies = [], []
        for s in range(2):
            core_copies[s].wait_recv()
            core_sum[s] = (parts[s, :, :, c].astype(F32) + core_in[s].astype(F32)).astype(BF16)
            x_copies.append(copy(core_sum.at[s, :, 1 - x], x_in.at[s], x_sems, (s,), x_peer))
            x_copies[s].start()
            grad(s)
        for s in range(2):
            x_copies[s].wait_recv()
            x_sum[s] = (core_sum[s, :, x].astype(F32) + x_in[s].astype(F32)).astype(BF16)
            z_copies.append({})
            for k in range(1, A):
                z_copies[s][k] = copy(
                    x_sum.at[s, (a + k) % A], z_in.at[s, k], z_sems, (s, k), far[k]
                )
                z_copies[s][k].start()
        for s in range(2):
            total = x_sum[s, a].astype(F32)
            for k in range(1, A):
                z_copies[s][k].wait_recv()
                total = total + z_in[s, k].astype(F32)
            column = sides[s][8]
            weight_out[:, column * width:(column + 1) * width] = total
            sent += z_copies[s].values()
        sent += core_copies + x_copies
    for one in sent:
        one.wait_send()


def body(image_feats, text_feats, image_proj, text_proj, pair_ids, log_temp, bias, loss_grad):
    n = lax.axis_size("loop")
    A = n // B
    rows, depth = image_feats.shape
    width = image_proj.shape[1]
    piece = depth // n
    scatter = depth % n == 0 and piece % 16 == 0
    cut = piece if scatter else 16
    vmem = pl.BlockSpec(memory_space=pltpu.VMEM)
    smem = pl.BlockSpec(memory_space=pltpu.SMEM)
    dma = pltpu.SemaphoreType.DMA
    lead = A if scatter else 1
    image_grad, text_grad, weight = pl.pallas_call(
        functools.partial(kernel, n, scatter),
        out_shape=(
            jax.ShapeDtypeStruct((rows, depth), BF16),
            jax.ShapeDtypeStruct((rows, depth), BF16),
            jax.ShapeDtypeStruct((piece if scatter else depth, 2 * width), F32),
        ),
        in_specs=[smem] * 3 + [vmem] * 5,
        out_specs=(vmem,) * 3,
        scratch_shapes=[
            pltpu.VMEM((B, rows, width), BF16),
            pltpu.VMEM((A, rows, width), BF16),
            pltpu.VMEM((B, 1, rows), jnp.int32),
            pltpu.VMEM((A, 1, rows), jnp.int32),
            pltpu.VMEM((B, rows, width), BF16),
            pltpu.VMEM((B, rows, width), BF16),
            pltpu.VMEM((A, rows, width), BF16),
            pltpu.VMEM((A, rows, width), BF16),
            pltpu.VMEM((2, lead, 2, 2, cut, width), BF16),
            pltpu.VMEM((2, lead, 2, cut, width), BF16),
            pltpu.VMEM((2, lead, 2, cut, width), BF16),
            pltpu.VMEM((2, lead, cut, width), BF16),
            pltpu.VMEM((2, lead, cut, width), BF16),
            pltpu.VMEM((2, lead, cut, width), BF16),
            dma((2, B)),
            dma((2, A)),
            dma((2, B)),
            dma((2, A)),
            dma((2, B)),
            dma((2, A)),
            dma((2, 2)),
            dma((2, 2)),
            dma((2, 2, A)),
        ],
        compiler_params=pltpu.CompilerParams(
            collective_id=0, has_side_effects=True, vmem_limit_bytes=48 * 1024 * 1024
        ),
    )(
        log_temp, bias, loss_grad, image_feats, text_feats, image_proj, text_proj,
        pair_ids.reshape(1, rows),
    )
    if not scatter:
        weight = lax.psum_scatter(weight, "loop", scatter_dimension=0, tiled=True)
    return image_grad, text_grad, weight


def solution(mesh):
    split = P(("groups", "loop"), None)
    return jax.shard_map(
        body,
        mesh=mesh,
        in_specs=(split, split, P(), P(), P(("groups", "loop")), P(), P(), P()),
        out_specs=(split, split, split),
        check_vma=False,
    )
```

time: 240 us -> 40.6 us (0.17)
  waiting for transfers between devices: 159 us -> 0 us
  matrix products: 54.2 us -> 0 us
  Pallas kernels: 0 us -> 31.2 us
  between operations: 16.2 us -> 2.59 us
  starting transfers between devices: 5.64 us -> 0 us
  local copies, waits for them, and re-layouts: 2.86 us -> 6.49 us
    ppermute x45 -> x0, waiting for transfers between devices: 104 us -> none  [shifted(): return lax.ppermute(block, axis, route)]
    unnamed x2 -> x0, waiting for transfers between devices: 55.1 us -> none
    dot_general x38 -> x0, matrix products: 54.2 us -> none  [the longest x32 48.9 us: tile_term(): return jnp.dot(coeff, other_half, preferred_element_type=jnp.float32)]
    pallas_call x0 -> x1, Pallas kernels: none -> 31.2 us  [body(): pl.pallas_call(functools.partial(kernel, n, scatter), out_shape=(jax.Shap...]
    ppermute x45 -> x0, starting transfers between devices: 5.61 us -> none  [shifted(): return lax.ppermute(block, axis, route)]
    unnamed x14 -> x13, local copies, waits for them, and re-layouts: 2.67 us -> 6.49 us
  transfers between devices with their start and end apart: 46 -> 0, of which waited for: 16 -> 0; matrix products, arithmetic and copies ran while one was open for 1% -> 0% of each run, Pallas kernels for 0% -> 0%
where the time goes in v1:
time: 40.6 us; the launch traced here: 40.3 us
  Pallas kernels  31.2 us (77%)
  local copies, waits for them, and re-layouts  6.49 us (16%)
  between operations  2.59 us (6%)
    pallas_call x1, Pallas kernels, body(): pl.pallas_call(functools.partial(kernel, n, scatter), out_shape=(jax.Shap...  31.2 us
    unnamed x13, local copies, waits for them, and re-layouts  6.49 us

profile of v1, /device:TPU:0, one launch (start us, length us, event | category | flops | bytes accessed | tf_op | source)
XLA Modules:
  0.0 40.3 jit_solution(2144637454328872894)
XLA Ops:
  2.6 0.0 copy-start.4
  2.6 0.6 %copy-done.4 = s32[128]{0:T(128)S(1)} copy-done((s32[128]{0:T(128)S(1)}, s32[128]{0:T(128)}, u32[]{:S(2)}) %copy-start.4) | copy-done | bytes 536
  3.2 0.0 copy-start
  3.2 1.0 %copy-done = bf16[768,256]{1,0:T(8,128)(2,1)S(1)} copy-done((bf16[768,256]{1,0:T(8,128)(2,1)S(1)}, bf16[768,256]{1,0:T(8,128)(2,1)}, u32[]{:S(2)}) %copy-start) | copy-done | bytes 393240
  4.2 0.0 copy-start.1
  4.2 1.0 %copy-done.1 = bf16[768,256]{1,0:T(8,128)(2,1)S(1)} copy-done((bf16[768,256]{1,0:T(8,128)(2,1)S(1)}, bf16[768,256]{1,0:T(8,128)(2,1)}, u32[]{:S(2)}) %copy-start.1) | copy-done | bytes 393240
  5.2 0.0 copy-start.2
  5.2 0.9 %copy-done.2 = bf16[128,768]{1,0:T(8,128)(2,1)S(1)} copy-done((bf16[128,768]{1,0:T(8,128)(2,1)S(1)}, bf16[128,768]{1,0:T(8,128)(2,1)}, u32[]{:S(2)}) %copy-start.2) | copy-done | bytes 196632
  6.1 0.0 copy-start.3
  6.1 0.9 %copy-done.3 = bf16[128,768]{1,0:T(8,128)(2,1)S(1)} copy-done((bf16[128,768]{1,0:T(8,128)(2,1)S(1)}, bf16[128,768]{1,0:T(8,128)(2,1)}, u32[]{:S(2)}) %copy-start.3) | copy-done | bytes 196632
  7.1 31.2 %shard_map.103 = (bf16[128,768]{1,0:T(8,128)(2,1)S(1)}, bf16[128,768]{1,0:T(8,128)(2,1)S(1)}, f32[48,512]{1,0:T(8,128)S(1)}) custom-call(f32[1]{0:T(128)S(6)} %copy.14.log_temp, f32[1]{0:T(128)S(6)} %copy.15.bias, f32[1]{0:T(128)S(6)} %copy.16.loss_grad, bf16[128,768]{1,0:T(8,128)(2,1)S(1)} %copy-done.2, bf16[128,768]{1,0:T(8,128)(2,1)S(1)} %copy-done.3, ...), custom_call_target="tpu_custom_call" | custom-call | tf_op jit(solution)/shard_map/pallas_call | solution.py:207
  38.3 0.7 %copy.17 = bf16[128,768]{1,0:T(8,128)(2,1)} copy(bf16[128,768]{1,0:T(8,128)(2,1)S(1)} %get-tuple-element.6) | data formatting | bytes 393216
  39.0 0.7 %copy.18 = bf16[128,768]{1,0:T(8,128)(2,1)} copy(bf16[128,768]{1,0:T(8,128)(2,1)S(1)} %get-tuple-element.7) | data formatting | bytes 393216
  39.6 0.6 %copy.19 = f32[48,512]{1,0:T(8,128)} copy(f32[48,512]{1,0:T(8,128)S(1)} %get-tuple-element.8) | data formatting | bytes 196608
Async XLA Ops:
  2.6 0.7 %copy-start.4 = (s32[128]{0:T(128)S(1)}, s32[128]{0:T(128)}, u32[]{:S(2)}) copy-start(s32[128]{0:T(128)} %param.12) | copy-start | bytes 1540
  3.2 1.0 %copy-start = (bf16[768,256]{1,0:T(8,128)(2,1)S(1)}, bf16[768,256]{1,0:T(8,128)(2,1)}, u32[]{:S(2)}) copy-start(bf16[768,256]{1,0:T(8,128)(2,1)} %image_proj.1) | copy-start | bytes 1179652
  4.2 1.0 %copy-start.1 = (bf16[768,256]{1,0:T(8,128)(2,1)S(1)}, bf16[768,256]{1,0:T(8,128)(2,1)}, u32[]{:S(2)}) copy-start(bf16[768,256]{1,0:T(8,128)(2,1)} %text_proj.1) | copy-start | bytes 1179652
  5.2 0.9 %copy-start.2 = (bf16[128,768]{1,0:T(8,128)(2,1)S(1)}, bf16[128,768]{1,0:T(8,128)(2,1)}, u32[]{:S(2)}) copy-start(bf16[128,768]{1,0:T(8,128)(2,1)} %image_feats.1) | copy-start | bytes 589828
  6.1 0.9 %copy-start.3 = (bf16[128,768]{1,0:T(8,128)(2,1)S(1)}, bf16[128,768]{1,0:T(8,128)(2,1)}, u32[]{:S(2)}) copy-start(bf16[128,768]{1,0:T(8,128)(2,1)} %text_feats.1) | copy-start | bytes 589828

commit v2 on v1

--- a/solution.py
+++ b/solution.py
@@ -8,6 +8,7 @@
 from jax.sharding import PartitionSpec as P
 
 B = 4
+VMEM_BYTES = 64000 * 1024
 F32 = jnp.float32
 BF16 = jnp.bfloat16
 
@@ -28,10 +29,12 @@
 
 def kernel(
     n, scatter,
-    log_temp, bias, loss_grad, image_feats, text_feats, image_proj, text_proj, ids,
-    image_grad, text_grad, weight_out,
+    log_temp, bias, loss_grad, image_feats_hbm, text_feats_hbm, image_proj_hbm, text_proj_hbm, ids,
+    image_grad_hbm, text_grad_hbm, weight_hbm,
     image_all, text_all, image_ids, text_ids, image_out, image_back, text_out, text_back,
     parts, core_in, core_sum, x_in, x_sum, z_in,
+    image_feats, text_feats, image_proj, text_proj, image_turned, text_turned, load_sems,
+    image_grad, text_grad, weight_out, store_sems,
     image_sems, text_sems, image_id_sems, text_id_sems, image_back_sems, text_back_sems,
     core_sems, x_sems, z_sems,
 ):
@@ -42,8 +45,20 @@
     x, c = b // 2, b % 2
     near = [a * B + (b + k) % B for k in range(B)]
     near_back = [a * B + (b + B - k) % B for k in range(B)]
-    far = [(a + k) % A * B + b for k in range(A)]
-    far_back = [(a + A - k) % A * B + b for k in range(A)]
+    if A == 4:
+        swap = [
+            a,
+            a + 1 - 2 * (a % 2),
+            (a + 2) % 4,
+            3 - a,
+        ]
+        far_a = far_a_back = swap
+    else:
+        far_a = [(a + k) % A for k in range(A)]
+        far_a_back = [(a + A - k) % A for k in range(A)]
+    far = [one * B + b for one in far_a]
+    far_back = [one * B + b for one in far_a_back]
+    far_first = [*range(2, A), 1]
     core_peer = a * B + x * 2 + (1 - c)
     x_peer = a * B + (1 - x) * 2 + c
 
@@ -53,6 +68,18 @@
             device_id={"loop": to}, device_id_type=pl.DeviceIdType.MESH,
         )
 
+    loads = [
+        pltpu.make_async_copy(src, dst, load_sems.at[i])
+        for i, (src, dst) in enumerate((
+            (text_feats_hbm, text_feats),
+            (text_proj_hbm, text_proj),
+            (ids, text_ids.at[0]),
+            (image_feats_hbm, image_feats),
+            (image_proj_hbm, image_proj),
+        ))
+    ]
+    for load in loads:
+        load.start()
     barrier = pltpu.get_barrier_semaphore()
     for to in near[1:] + far[1:]:
         pl.semaphore_signal(
@@ -63,30 +90,35 @@
     bias_v = bias[0]
     scale = loss_grad[0]
 
+    sent = []
+    image_copies, text_copies, image_id_copies, text_id_copies = {}, {}, {}, {}
+
+    for load in loads[:3]:
+        load.wait()
+    text_unit, text_norm = unit_rows(dot(text_feats[...], text_proj[...], ((1,), (0,))))
+    text_all[0] = text_unit.astype(BF16)
+    pl.semaphore_wait(barrier, A + B - 2)
+    for k in far_first:
+        text_copies[k] = copy(text_all.at[0], text_all.at[k], text_sems, (k,), far[k])
+        text_copies[k].start()
+    for load in loads[3:]:
+        load.wait()
     image_unit, image_norm = unit_rows(dot(image_feats[...], image_proj[...], ((1,), (0,))))
     image_all[0] = image_unit.astype(BF16)
-    text_unit, text_norm = unit_rows(dot(text_feats[...], text_proj[...], ((1,), (0,))))
-    text_all[0] = text_unit.astype(BF16)
-    image_ids[0] = ids[...]
-    text_ids[0] = ids[...]
-    pl.semaphore_wait(barrier, A + B - 2)
-
-    sent = []
-    image_copies, text_copies, image_id_copies, text_id_copies = {}, {}, {}, {}
-    for k in range(1, A):
-        text_copies[k] = copy(text_all.at[0], text_all.at[k], text_sems, (k,), far[k])
-        text_copies[k].start()
     for k in range(1, B):
         image_copies[k] = copy(image_all.at[0], image_all.at[k], image_sems, (k,), near[k])
         image_copies[k].start()
     for k in range(1, B):
-        image_id_copies[k] = copy(image_ids.at[0], image_ids.at[k], image_id_sems, (k,), near[k])
+        image_id_copies[k] = copy(text_ids.at[0], image_ids.at[k], image_id_sems, (k,), near[k])
         image_id_copies[k].start()
     for k in range(1, A):
         text_id_copies[k] = copy(text_ids.at[0], text_ids.at[k], text_id_sems, (k,), far[k])
         text_id_copies[k].start()
     sent += [*text_copies.values(), *image_copies.values()]
     sent += [*image_id_copies.values(), *text_id_copies.values()]
+    image_ids[0] = text_ids[0]
+    text_turned[...] = text_feats[...].T
+    image_turned[...] = image_feats[...].T
 
     for k in range(1, B):
         image_copies[k].wait_recv()
@@ -135,8 +167,8 @@
         return temp * total
 
     sides = (
-        (text_feats, text_unit, text_norm, text_own, back, text_back, text_proj, text_grad, 1),
-        (image_feats, image_unit, image_norm, image_acc[:rows], image_back_copies, image_back,
+        (text_turned, text_unit, text_norm, text_own, back, text_back, text_proj, text_grad, 1),
+        (image_turned, image_unit, image_norm, image_acc[:rows], image_back_copies, image_back,
          image_proj, image_grad, 0),
     )
     width = image_all.shape[2]
@@ -145,7 +177,7 @@
     for s, (feats, unit, norm, own, copies, ref, _, _, column) in enumerate(sides):
         raw = raw_grad_of(unit, norm, reduced(own, copies, ref))
         raws.append(raw)
-        part = dot(feats[...], raw, ((0,), (0,)))
+        part = dot(feats[...], raw, ((1,), (0,)))
         if scatter:
             parts[s] = part.astype(BF16).reshape(parts.shape[1:])
             core_copies.append(
@@ -155,9 +187,17 @@
         else:
             weight_out[:, column * width:(column + 1) * width] = part
 
+    stores = [
+        pltpu.make_async_copy(src, dst, store_sems.at[i])
+        for i, (src, dst) in enumerate((
+            (text_grad, text_grad_hbm), (image_grad, image_grad_hbm), (weight_out, weight_hbm),
+        ))
+    ]
+
     def grad(s):
         proj, out = sides[s][6:8]
         out[...] = dot(raws[s], proj[...], ((1,), (1,))).astype(BF16)
+        stores[s].start()
 
     if not scatter:
         grad(0)
@@ -174,9 +214,9 @@
             x_copies[s].wait_recv()
             x_sum[s] = (core_sum[s, :, x].astype(F32) + x_in[s].astype(F32)).astype(BF16)
             z_copies.append({})
-            for k in range(1, A):
+            for k in far_first:
                 z_copies[s][k] = copy(
-                    x_sum.at[s, (a + k) % A], z_in.at[s, k], z_sems, (s, k), far[k]
+                    x_sum.at[s, far_a[k]], z_in.at[s, k], z_sems, (s, k), far[k]
                 )
                 z_copies[s][k].start()
         for s in range(2):
@@ -188,8 +228,20 @@
             weight_out[:, column * width:(column + 1) * width] = total
             sent += z_copies[s].values()
         sent += core_copies + x_copies
+    stores[2].start()
     for one in sent:
         one.wait_send()
+    for one in stores:
+        one.wait()
+
+
+def store(image_in, text_in, weight_in, image_grad, text_grad, weight_out, sems):
+    pairs = ((image_in, image_grad), (text_in, text_grad), (weight_in, weight_out))
+    copies = [pltpu.make_async_copy(*pair, sems.at[i]) for i, pair in enumerate(pairs)]
+    for one in copies:
+        one.start()
+    for one in copies:
+        one.wait()
 
 
 def body(image_feats, text_feats, image_proj, text_proj, pair_ids, log_temp, bias, loss_grad):
@@ -200,7 +252,7 @@
     piece = depth // n
     scatter = depth % n == 0 and piece % 16 == 0
     cut = piece if scatter else 16
-    vmem = pl.BlockSpec(memory_space=pltpu.VMEM)
+    hbm = pl.BlockSpec(memory_space=pltpu.HBM)
     smem = pl.BlockSpec(memory_space=pltpu.SMEM)
     dma = pltpu.SemaphoreType.DMA
     lead = A if scatter else 1
@@ -211,8 +263,8 @@
             jax.ShapeDtypeStruct((rows, depth), BF16),
             jax.ShapeDtypeStruct((piece if scatter else depth, 2 * width), F32),
         ),
-        in_specs=[smem] * 3 + [vmem] * 5,
-        out_specs=(vmem,) * 3,
+        in_specs=[smem] * 3 + [hbm] * 5,
+        out_specs=(hbm,) * 3,
         scratch_shapes=[
             pltpu.VMEM((B, rows, width), BF16),
             pltpu.VMEM((A, rows, width), BF16),
@@ -228,6 +280,17 @@
             pltpu.VMEM((2, lead, cut, width), BF16),
             pltpu.VMEM((2, lead, cut, width), BF16),
             pltpu.VMEM((2, lead, cut, width), BF16),
+            pltpu.VMEM((rows, depth), BF16),
+            pltpu.VMEM((rows, depth), BF16),
+            pltpu.VMEM((depth, width), BF16),
+            pltpu.VMEM((depth, width), BF16),
+            pltpu.VMEM((depth, rows), BF16),
+            pltpu.VMEM((depth, rows), BF16),
+            dma((5,)),
+            pltpu.VMEM((rows, depth), BF16),
+            pltpu.VMEM((rows, depth), BF16),
+            pltpu.VMEM((piece if scatter else depth, 2 * width), F32),
+            dma((3,)),
             dma((2, B)),
             dma((2, A)),
             dma((2, B)),
@@ -239,14 +302,23 @@
             dma((2, 2, A)),
         ],
         compiler_params=pltpu.CompilerParams(
-            collective_id=0, has_side_effects=True, vmem_limit_bytes=48 * 1024 * 1024
+            collective_id=0, has_side_effects=True, vmem_limit_bytes=VMEM_BYTES
         ),
     )(
         log_temp, bias, loss_grad, image_feats, text_feats, image_proj, text_proj,
         pair_ids.reshape(1, rows),
     )
-    if not scatter:
-        weight = lax.psum_scatter(weight, "loop", scatter_dimension=0, tiled=True)
+    results = (image_grad, text_grad, weight)
+    if scatter:
+        return pl.pallas_call(
+            store,
+            out_shape=tuple(jax.ShapeDtypeStruct(one.shape, one.dtype) for one in results),
+            in_specs=[hbm] * 3,
+            out_specs=(hbm,) * 3,
+            scratch_shapes=[dma((3,))],
+            compiler_params=pltpu.CompilerParams(vmem_limit_bytes=VMEM_BYTES),
+        )(*results)
+    weight = lax.psum_scatter(weight, "loop", scatter_dimension=0, tiled=True)
     return image_grad, text_grad, weight
 
 

time: 40.6 us -> 50.7 us (1.25)
  Pallas kernels: 31.2 us -> 47.9 us
  local copies, waits for them, and re-layouts: 6.49 us -> 0 us
    pallas_call x0 -> x1, Pallas kernels: none -> 16 us  [body(): pl.pallas_call(store, out_shape=tuple((jax.ShapeDtypeStruct(one.shape, on...]
    unnamed x13 -> x0, local copies, waits for them, and re-layouts: 6.49 us -> none
    pallas_call x1, Pallas kernels: 31.2 us -> 31.9 us  [body(): pl.pallas_call(functools.partial(kernel, n, scatter), out_shape=(jax.Shap...]
where the time goes in v2:
time: 50.7 us; the launch traced here: 50.5 us
  Pallas kernels  47.9 us (94%)
  between operations  2.58 us (5%)
    pallas_call x1, Pallas kernels, body(): pl.pallas_call(functools.partial(kernel, n, scatter), out_shape=(jax.Shap...  31.9 us
    pallas_call x1, Pallas kernels, body(): pl.pallas_call(store, out_shape=tuple((jax.ShapeDtypeStruct(one.shape, on...  16 us

profile of v2, /device:TPU:0, one launch (start us, length us, event | category | flops | bytes accessed | tf_op | source)
XLA Modules:
  0.0 50.5 jit_solution(4686666759305586022)
XLA Ops:
  2.6 31.9 %shard_map.103 = (bf16[128,768]{1,0:T(8,128)(2,1)}, bf16[128,768]{1,0:T(8,128)(2,1)}, f32[48,512]{1,0:T(8,128)}) custom-call(f32[1]{0:T(128)S(6)} %copy.11.log_temp, f32[1]{0:T(128)S(6)} %copy.12.bias, f32[1]{0:T(128)S(6)} %copy.13.loss_grad, bf16[128,768]{1,0:T(8,128)(2,1)} %image_feats_hbm.1, bf16[128,768]{1,0:T(8,128)(2,1)} %text_feats_hbm.1, ...), custom_call_target="tpu_custom_call" | custom-call | tf_op jit(solution)/shard_map/pallas_call | solution.py:259
  34.5 16.0 %shard_map.104 = (bf16[128,768]{1,0:T(8,128)(2,1)}, bf16[128,768]{1,0:T(8,128)(2,1)}, f32[48,512]{1,0:T(8,128)}) custom-call(bf16[128,768]{1,0:T(8,128)(2,1)} %get-tuple-element.6.image_in, bf16[128,768]{1,0:T(8,128)(2,1)} %get-tuple-element.7.text_in, f32[48,512]{1,0:T(8,128)} %get-tuple-element.8.weight_in), custom_call_target="tpu_custom_call" | custom-call | tf_op jit(solution)/shard_map/pallas_call | solution.py:313

commit v3 on v2

--- a/solution.py
+++ b/solution.py
@@ -235,12 +235,19 @@
         one.wait()
 
 
-def store(image_in, text_in, weight_in, image_grad, text_grad, weight_out, sems):
-    pairs = ((image_in, image_grad), (text_in, text_grad), (weight_in, weight_out))
-    copies = [pltpu.make_async_copy(*pair, sems.at[i]) for i, pair in enumerate(pairs)]
-    for one in copies:
+def store(
+    image_in, text_in, weight_in, image_grad, text_grad, weight_out, image_buf, text_buf, weight_buf, sems
+):
+    sources, targets = (image_in, text_in, weight_in), (image_grad, text_grad, weight_out)
+    buffers = (image_buf, text_buf, weight_buf)
+    loads = [pltpu.make_async_copy(sources[i], buffers[i], sems.at[0, i]) for i in range(3)]
+    stores = [pltpu.make_async_copy(buffers[i], targets[i], sems.at[1, i]) for i in range(3)]
+    for one in loads:
         one.start()
-    for one in copies:
+    for load, one in zip(loads, stores):
+        load.wait()
+        one.start()
+    for one in stores:
         one.wait()
 
 
@@ -315,7 +322,7 @@
             out_shape=tuple(jax.ShapeDtypeStruct(one.shape, one.dtype) for one in results),
             in_specs=[hbm] * 3,
             out_specs=(hbm,) * 3,
-            scratch_shapes=[dma((3,))],
+            scratch_shapes=[pltpu.VMEM(one.shape, one.dtype) for one in results] + [dma((2, 3))],
             compiler_params=pltpu.CompilerParams(vmem_limit_bytes=VMEM_BYTES),
         )(*results)
     weight = lax.psum_scatter(weight, "loop", scatter_dimension=0, tiled=True)

time: 50.7 us -> 36.4 us (0.72)
  Pallas kernels: 47.9 us -> 33.7 us
    pallas_call x1, Pallas kernels: 16 us -> 1.78 us  [body(): pl.pallas_call(store, out_shape=tuple((jax.ShapeDtypeStruct(one.shape, on...]
where the time goes in v3:
time: 36.4 us; the launch traced here: 36.3 us
  Pallas kernels  33.7 us (93%)
  between operations  2.58 us (7%)
    pallas_call x1, Pallas kernels, body(): pl.pallas_call(functools.partial(kernel, n, scatter), out_shape=(jax.Shap...  31.9 us
    pallas_call x1, Pallas kernels, body(): pl.pallas_call(store, out_shape=tuple((jax.ShapeDtypeStruct(one.shape, on...  1.78 us

profile of v3, /device:TPU:0, one launch (start us, length us, event | category | flops | bytes accessed | tf_op | source)
XLA Modules:
  0.0 36.3 jit_solution(5555319955901307910)
XLA Ops:
  2.6 31.9 %shard_map.103 = (bf16[128,768]{1,0:T(8,128)(2,1)}, bf16[128,768]{1,0:T(8,128)(2,1)}, f32[48,512]{1,0:T(8,128)}) custom-call(f32[1]{0:T(128)S(6)} %copy.11.log_temp, f32[1]{0:T(128)S(6)} %copy.12.bias, f32[1]{0:T(128)S(6)} %copy.13.loss_grad, bf16[128,768]{1,0:T(8,128)(2,1)} %image_feats_hbm.1, bf16[128,768]{1,0:T(8,128)(2,1)} %text_feats_hbm.1, ...), custom_call_target="tpu_custom_call" | custom-call | tf_op jit(solution)/shard_map/pallas_call | solution.py:266
  34.5 1.8 %shard_map.104 = (bf16[128,768]{1,0:T(8,128)(2,1)}, bf16[128,768]{1,0:T(8,128)(2,1)}, f32[48,512]{1,0:T(8,128)}) custom-call(bf16[128,768]{1,0:T(8,128)(2,1)} %get-tuple-element.6.image_in, bf16[128,768]{1,0:T(8,128)(2,1)} %get-tuple-element.7.text_in, f32[48,512]{1,0:T(8,128)} %get-tuple-element.8.weight_in), custom_call_target="tpu_custom_call" | custom-call | tf_op jit(solution)/shard_map/pallas_call | solution.py:320

commit v4 on v3

--- a/solution.py
+++ b/solution.py
@@ -99,6 +99,8 @@
     text_all[0] = text_unit.astype(BF16)
     pl.semaphore_wait(barrier, A + B - 2)
     for k in far_first:
+        if A == 4 and k == 3:
+            continue
         text_copies[k] = copy(text_all.at[0], text_all.at[k], text_sems, (k,), far[k])
         text_copies[k].start()
     for load in loads[3:]:
@@ -114,7 +116,7 @@
     for k in range(1, A):
         text_id_copies[k] = copy(text_ids.at[0], text_ids.at[k], text_id_sems, (k,), far[k])
         text_id_copies[k].start()
-    sent += [*text_copies.values(), *image_copies.values()]
+    sent += [*image_copies.values()]
     sent += [*image_id_copies.values(), *text_id_copies.values()]
     image_ids[0] = text_ids[0]
     text_turned[...] = text_feats[...].T
@@ -132,23 +134,30 @@
     text_own = None
     back = {}
     for k in [0, *range(1, A)]:
+        if A == 4 and k == 1:
+            text_copies[2].wait_recv()
+            text_copies[3] = copy(text_all.at[2], text_all.at[3], text_sems, (3,), far[1])
+            text_copies[3].start()
         if k:
-            text_copies[k].wait_recv()
+            if A != 4 or k != 2:
+                text_copies[k].wait_recv()
             text_id_copies[k].wait_recv()
         texts = text_all[k]
         logits = temp * dot(images, texts, ((1,), (1,))) + bias_v
         equal = (image_keys == text_ids[k].astype(F32)).astype(F32)
         coeff = (scale * (jax.nn.sigmoid(logits) - equal)).astype(BF16)
         term = dot(coeff, images, ((0,), (0,)))
-        if k:
+        if A == 4 and k == 2:
+            crossing = term
+        elif k:
             text_out[k] = term.astype(BF16)
-            back[k] = copy(text_out.at[k], text_back.at[k], text_back_sems, (k,), far_back[k])
+            back[k] = copy(text_out.at[k], text_back.at[k], text_back_sems, (k,), far[1] if A == 4 else far_back[k])
             back[k].start()
         else:
             text_own = term
         term = dot(coeff, texts, ((1,), (0,)))
         image_acc = term if image_acc is None else image_acc + term
-    sent += back.values()
+    sent += text_copies.values()
 
     image_back_copies = {}
     for k in range(1, B):
@@ -158,6 +167,14 @@
         )
         image_back_copies[k].start()
     sent += image_back_copies.values()
+    sent += back.values()
+    if A == 4:
+        back[3].wait_recv()
+        text_out[2] = (crossing + text_back[3].astype(F32)).astype(BF16)
+        back[2] = copy(text_out.at[2], text_back.at[2], text_back_sems, (2,), far[2])
+        back[2].start()
+        sent.append(back[2])
+        del back[3]
 
     def reduced(own, copies, ref):
         total = own

time: 36.4 us -> 39.5 us (1.085)
  Pallas kernels: 33.7 us -> 36.7 us
    pallas_call x1, Pallas kernels: 31.9 us -> 34.9 us  [body(): pl.pallas_call(functools.partial(kernel, n, scatter), out_shape=(jax.Shap...]
where the time goes in v4:
time: 39.5 us; the launch traced here: 39.3 us
  Pallas kernels  36.7 us (93%)
  between operations  2.58 us (7%)
    pallas_call x1, Pallas kernels, body(): pl.pallas_call(functools.partial(kernel, n, scatter), out_shape=(jax.Shap...  34.9 us
    pallas_call x1, Pallas kernels, body(): pl.pallas_call(store, out_shape=tuple((jax.ShapeDtypeStruct(one.shape, on...  1.78 us

profile of v4, /device:TPU:0, one launch (start us, length us, event | category | flops | bytes accessed | tf_op | source)
XLA Modules:
  0.0 39.3 jit_solution(8009159258865423986)
XLA Ops:
  2.6 34.9 %shard_map.103 = (bf16[128,768]{1,0:T(8,128)(2,1)}, bf16[128,768]{1,0:T(8,128)(2,1)}, f32[48,512]{1,0:T(8,128)}) custom-call(f32[1]{0:T(128)S(6)} %copy.11.log_temp, f32[1]{0:T(128)S(6)} %copy.12.bias, f32[1]{0:T(128)S(6)} %copy.13.loss_grad, bf16[128,768]{1,0:T(8,128)(2,1)} %image_feats_hbm.1, bf16[128,768]{1,0:T(8,128)(2,1)} %text_feats_hbm.1, ...), custom_call_target="tpu_custom_call" | custom-call | tf_op jit(solution)/shard_map/pallas_call | solution.py:283
  37.5 1.8 %shard_map.104 = (bf16[128,768]{1,0:T(8,128)(2,1)}, bf16[128,768]{1,0:T(8,128)(2,1)}, f32[48,512]{1,0:T(8,128)}) custom-call(bf16[128,768]{1,0:T(8,128)(2,1)} %get-tuple-element.6.image_in, bf16[128,768]{1,0:T(8,128)(2,1)} %get-tuple-element.7.text_in, f32[48,512]{1,0:T(8,128)} %get-tuple-element.8.weight_in), custom_call_target="tpu_custom_call" | custom-call | tf_op jit(solution)/shard_map/pallas_call | solution.py:337
